TPU v7x, 32 devices: a whole 2x2x4 slice. The times are simulated.
32 devices in a mesh: dp: 4 (over y, core), mp: 8 (over z, x).
Axes of the slice: x: 2, y: 2, z: 4, core: 2. Of those that a mesh axis runs over, the one named last changes fastest.
Arguments:
- layer_input: bfloat16 [2048, 4096], P('dp', 'mp'), may hold values from -6 to 6
- gate_pre: bfloat16 [2048, 14336], P('dp', 'mp'), may hold values from -6 to 6
- up_pre: bfloat16 [2048, 14336], P('dp', 'mp'), may hold values from -6 to 6
- out_grad: bfloat16 [2048, 4096], P('dp', 'mp'), may hold values from -36 to 36
- w_down: bfloat16 [14336, 4096], P('mp'), may hold values from -0.09375 to 0.09375
- proj_input: bfloat16 [4096, 64], P('mp'), may hold values from -4 to 4
- proj_hidden: bfloat16 [14336, 64], P('mp'), may hold values from -4 to 4
- proj_gate: bfloat16 [14336, 64], P('mp'), may hold values from -0.046875 to 0.046875
- proj_upward: bfloat16 [14336, 64], P('mp'), may hold values from -0.046875 to 0.046875
- proj_output: bfloat16 [64, 4096], P(None, 'mp'), may hold values from -0.09375 to 0.09375
- seq_ids: int32 [4, 512], P('dp'), may hold values from 0 to 7, never falling along the last dimension, each value on 1 to 128 neighbouring positions
Outputs:
- features: float32 [32, 3, 4096], P('dp', None, 'mp')
Inputs may be any that keep to these rules, and one draw needn't show every extreme that they name: `seq_ids`: within each row the ids never fall and every id appears; every sequence has 1 to 128 tokens and some sequence of each row has exactly 128.
All inputs are finite; a program needn't handle non-finite values.
Results may differ from a plain program's by a relative error of at most 0.0029.
Values may be sent and summed in bfloat16 or wider, within the bound.
A program may use at most 64 MiB of HBM per device.

v0:
```python
import jax
import jax.numpy as jnp
from jax import lax
from jax.sharding import PartitionSpec as P

SEQ_DEV = 8


def silu_parts(gate_value):
    sigmoid_v = jax.nn.sigmoid(gate_value)
    return (gate_value * sigmoid_v, sigmoid_v * (1.0 + gate_value * (1.0 - sigmoid_v)))


def layer_features(member, left_in, left_hid, gate_factor, up_factor, out_factor):
    seq_count = member.shape[0]
    tok_rows = member.shape[1]
    left_width = left_in.shape[1]
    rank_dim = out_factor.shape[1]
    weighted_in = (member[:, None, :] * left_in.T[None, :, :]).reshape(
        seq_count * left_width, tok_rows
    )
    weighted_hid = (member[:, None, :] * left_hid.T[None, :, :]).reshape(
        seq_count * left_width, tok_rows
    )
    paired = jnp.dot(
        weighted_in,
        jnp.concatenate([gate_factor, up_factor], axis=1),
        precision=lax.Precision.HIGHEST,
    )
    paired = paired.reshape(seq_count, left_width, 2, rank_dim)
    gate_feat = paired[:, :, 0, :].reshape(seq_count, left_width * rank_dim)
    up_feat = paired[:, :, 1, :].reshape(seq_count, left_width * rank_dim)
    down_feat = jnp.dot(weighted_hid, out_factor, precision=lax.Precision.HIGHEST).reshape(
        seq_count, left_width * rank_dim
    )
    return jnp.stack([gate_feat, up_feat, down_feat], axis=1)


def per_device(
    layer_input,
    gate_pre,
    up_pre,
    out_grad,
    w_down,
    proj_input,
    proj_hidden,
    proj_gate,
    proj_upward,
    proj_output,
    seq_ids,
):
    contract = (((1,), (1,)), ((), ()))
    rank_dim = proj_input.shape[1]
    own_width = rank_dim // lax.axis_size("mp")
    position = lax.axis_index("mp")
    gate_value = gate_pre.astype(jnp.float32)
    up_value = up_pre.astype(jnp.float32)
    activated, slope_value = silu_parts(gate_value)
    hidden = (activated * up_value).astype(jnp.bfloat16)
    in_part = jnp.dot(layer_input, proj_input, preferred_element_type=jnp.float32)
    hid_part = jnp.dot(hidden, proj_hidden, preferred_element_type=jnp.float32)
    hidden_grad = lax.dot_general(
        lax.all_gather(out_grad, "mp", axis=1, tiled=True),
        w_down,
        contract,
        preferred_element_type=jnp.float32,
    )
    out_part = lax.dot_general(out_grad, proj_output, contract, preferred_element_type=jnp.float32)
    gate_grad = (hidden_grad * up_value * slope_value).astype(jnp.bfloat16)
    upward_grad = (hidden_grad * activated).astype(jnp.bfloat16)
    gate_part = jnp.dot(gate_grad, proj_gate, preferred_element_type=jnp.float32)
    up_part = jnp.dot(upward_grad, proj_upward, preferred_element_type=jnp.float32)
    gate_part, up_part = (gate_part, up_part)
    in_factor, hid_factor, gate_factor, up_factor, out_factor = lax.psum(
        (in_part, hid_part, gate_part, up_part, out_part), "mp"
    )
    member = (seq_ids[0][None, :] == jnp.arange(SEQ_DEV, dtype=jnp.int32)[:, None]).astype(
        jnp.float32
    )
    own_in = lax.dynamic_slice_in_dim(in_factor, position * own_width, own_width, 1)
    own_hid = lax.dynamic_slice_in_dim(hid_factor, position * own_width, own_width, 1)
    raw_feat = layer_features(member, own_in, own_hid, gate_factor, up_factor, out_factor)
    squares = jnp.sum(raw_feat * raw_feat, axis=(0, 2))
    total_sq = lax.psum(squares, ("dp", "mp"))
    entries = raw_feat.shape[0] * lax.axis_size("dp") * rank_dim * rank_dim
    scale_value = lax.rsqrt(total_sq / entries + 1e-06)
    return raw_feat * scale_value[None, :, None]


def solution(mesh):
    in_specs = (
        P("dp", "mp"),
        P("dp", "mp"),
        P("dp", "mp"),
        P("dp", "mp"),
        P("mp", None),
        P("mp", None),
        P("mp", None),
        P("mp", None),
        P("mp", None),
        P(None, "mp"),
        P("dp", None),
    )
    out_specs = P("dp", None, "mp")
    return jax.shard_map(
        per_device, mesh=mesh, in_specs=in_specs, out_specs=out_specs, check_vma=False
    )
```

profile of v0, /device:TPU:0, one launch (start us, length us, event | category | flops | bytes accessed | tf_op | source)
XLA Modules:
  0.0 228.1 jit_solution(7332477301547251723)
XLA Ops:
  6.5 0.7 all-gather.2.cloned.1.call-update
  7.3 0.0 all-reduce.3.cloned.1.call-start
  7.3 0.3 copy-done
  7.6 1.8 fusion.28
  9.4 2.0 fusion.30
  11.4 4.0 %fusion.9 = f32[512,64]{0,1:T(8,128)} fusion(bf16[1792,64]{0,1:T(8,128)(2,1)} %param.17, bf16[512,1792]{1,0:T(8,128)(2,1)} %param.13, bf16[512,1792]{1,0:T(8,128)(2,1)} %param.12), kind=kOutput, calls=%fused_computation.15 | convolution fusion | flops 124780544 | bytes 4030464 | tf_op jit(solution)/shard_map/dot_general | solution.py:61
  15.3 71.8 %all-gather.2.cloned.1.call-done = bf16[512,4096]{1,0:T(8,128)(2,1)} async-done(((bf16[512,512]{1,0:T(8,128)(2,1)}), bf16[512,4096]{1,0:T(8,128)(2,1)}) %all-gather.2.cloned.1.call-update) | async-done | bytes 4194320 | tf_op jit(solution)/shard_map/all_gather | solution.py:63
  87.2 11.9 %fusion.29 = f32[512,1792]{1,0:T(8,128)S(1)} fusion(bf16[512,4096]{1,0:T(8,128)(2,1)} %all-gather.2.cloned.1.call-done, bf16[1792,4096]{1,0:T(8,128)(2,1)} %param.15), kind=kOutput, calls=%fused_computation.43 | convolution fusion | flops 7516192768 | bytes 22544384 | tf_op jit(solution)/shard_map/dot_general | solution.py:62
  99.1 0.0 copy-done.2
  99.1 0.0 copy-start.5
  99.1 2.3 %fusion.11 = f32[512,64]{0,1:T(8,128)} fusion(bf16[1792,64]{0,1:T(8,128)(2,1)S(1)} %copy-done.4, f32[512,1792]{1,0:T(8,128)S(1)} %fusion.29, bf16[512,1792]{1,0:T(8,128)(2,1)S(1)} %copy-done.2, bf16[512,1792]{1,0:T(8,128)(2,1)S(1)} %copy-done.3), kind=kOutput, calls=%fused_computation.16 | convolution fusion | flops 128450560 | bytes 7700480 | tf_op jit(solution)/shard_map/dot_general | solution.py:71
  101.4 1.8 fusion.8
  103.2 0.0 all-reduce.3.cloned.1.call-update
  103.3 74.0 %all-reduce.3.cloned.1.call-done = (f32[512,64]{0,1:T(8,128)}, f32[512,64]{0,1:T(8,128)}, f32[512,64]{0,1:T(8,128)}, f32[512,64]{1,0:T(8,128)}, f32[512,64]{0,1:T(8,128)}) async-done(((f32[512,64]{0,1:T(8,128)}, f32[512,64]{0,1:T(8,128)}, f32[512,64]{0,1:T(8,128)}, f32[512,64]{1,0:T(8,128)}, f32[512,64]{0,1:T(8,128)}), (f32[512,64]{0,1:T(8,128)}, f32[512,64]{0,1:T(8,128)}, f32[512,64]{0,1:T(8,128)}, ...) | async-done | bytes 655376 | tf_op jit(solution)/shard_map/psum | solution.py:74
  177.3 1.0 pad_maximum_fusion
  178.3 0.7 dynamic-slice_bitcast_fusion
  179.1 0.5 fusion.13
  179.6 0.1 stack_reshape_squeeze.6
  179.7 0.1 stack_reshape_squeeze.7
  179.7 1.2 fusion.15
  181.0 0.1 stack_reshape.3
  181.1 0.1 multiply_reduce_fusion
  181.2 39.4 %psum.47 = f32[3]{0:T(128)S(1)} all-reduce(f32[3]{0:T(128)S(1)} %multiply_reduce_fusion), channel_id=1, replica_groups=mesh['dp'=4,'mp'=8] {'dp','mp'}, use_global_device_ids=true, to_apply=%region_6.0 | all-reduce | flops 3 | bytes 24 | tf_op jit(solution)/shard_map/psum | solution.py:84
  220.6 0.7 broadcast_multiply_fusion
  (16 shorter events, 0.0 us)
Async XLA Ops:
  6.5 1.0 copy-start
  6.5 80.6 %all-gather.2.cloned.1.call-start = ((), (), s32[]{:S(2)}) async-start(), calls=%async_computation | async-start | bytes 4718592 | tf_op jit(solution)/shard_map/all_gather | solution.py:63
  7.3 170.1 %all-reduce.3.cloned.1.call-start = ((), (), s32[]{:S(2)}) async-start(), calls=%async_computation.1 | async-start | bytes 1572864 | tf_op jit(solution)/shard_map/psum | solution.py:74
  15.3 83.7 %copy-start.2 = (bf16[512,1792]{1,0:T(8,128)(2,1)S(1)}, bf16[512,1792]{1,0:T(8,128)(2,1)}, u32[]{:S(2)}) copy-start(bf16[512,1792]{1,0:T(8,128)(2,1)} %param.13) | copy-start | bytes 5505028
  15.3 83.7 %copy-start.4 = (bf16[1792,64]{0,1:T(8,128)(2,1)S(1)}, bf16[1792,64]{0,1:T(8,128)(2,1)}, u32[]{:S(2)}) copy-start(bf16[1792,64]{0,1:T(8,128)(2,1)} %param.18) | copy-start | bytes 688132
  87.2 11.9 %copy-start.3 = (bf16[512,1792]{1,0:T(8,128)(2,1)S(1)}, bf16[512,1792]{1,0:T(8,128)(2,1)}, u32[]{:S(2)}) copy-start(bf16[512,1792]{1,0:T(8,128)(2,1)} %param.12) | copy-start | bytes 5505028
  99.1 2.3 %copy-start.5 = (bf16[1792,64]{0,1:T(8,128)(2,1)S(1)}, bf16[1792,64]{0,1:T(8,128)(2,1)}, u32[]{:S(2)}) copy-start(bf16[1792,64]{0,1:T(8,128)(2,1)} %param.19) | copy-start | bytes 688132
  101.4 1.8 copy-start.1
Sparse Core Ops, SparseCore 0:
  9.4 77.7 all-gather.1
  103.4 73.9 all-reduce.2
where the time goes:
time: 229 us; the launch traced here: 228 us
  waiting for transfers between devices  147 us (64%)
  blocking collectives  39.4 us (17%)
  matrix products  25.5 us (11%)
  between operations  13.5 us (6%)
    psum x1, waiting for transfers between devices, per_device(): lax.psum((in_part, hid_part, gate_part, up_part, out_part), 'mp')  74 us
    all_gather x1, waiting for transfers between devices, per_device(): lax.all_gather(out_grad, 'mp', axis=1, tiled=True)  71.8 us
    psum x1, blocking collectives, per_device(): total_sq = lax.psum(squares, ('dp', 'mp'))  39.4 us
    dot_general x1, matrix products, per_device(): lax.dot_general(lax.all_gather(out_grad, 'mp', axis=1, tiled=True), w_dow...  11.9 us
  transfers between devices with their start and end apart: 2, of which 2 were waited for; matrix products, arithmetic and copies ran while one was open for 3% of the time, Pallas kernels for 0%

commit v1 on v0

--- a/solution.py
+++ b/solution.py
@@ -1,6 +1,10 @@
+import functools
+
 import jax
 import jax.numpy as jnp
 from jax import lax
+from jax.experimental import pallas as pl
+from jax.experimental.pallas import tpu as pltpu
 from jax.sharding import PartitionSpec as P
 
 SEQ_DEV = 8
@@ -87,7 +91,441 @@
     return raw_feat * scale_value[None, :, None]
 
 
+MESH = pl.DeviceIdType.MESH
+ROWS_Z, COLS_X = 4, 2
+PIECES = 4
+X_FIRST = 0
+TILE = 256
+ROWS = 128
+NT = (((1,), (1,)), ((), ()))
+UP, DOWN, ACROSS = 0, 1, 2
+
+
+def fused_kernel(
+    ndp, nmp,
+    x_hbm, gate_hbm, up_hbm, grad_hbm, w_hbm, pin_hbm, phid_hbm, pgate_hbm, pup_hbm, pout_hbm, seq_hbm,
+    out_ref,
+    x_v, gate_v, up_v, grad_v, w_v, pin_v, phid_v, pgate_v, pup_v, pout_v, seq_v,
+    hgrad, act, upslope, hid_tile, up_tile, acc_a, acc_b,
+    fac_send, fac_recv, full, weighted, raw_own, raw_send, raw_recv,
+    sq_mine, sq_recv, sq_group, sq_dp,
+    load_sem, w_sem, g_send, g_recv, fac_ss, fac_rs, full_ss, full_rs, raw_ss, raw_rs,
+    sq_ss, sq_rs, dp_ss, dp_rs,
+):
+    dp = lax.axis_index("dp")
+    me = lax.axis_index("mp")
+    z, x = me // COLS_X, lax.rem(me, COLS_X)
+    xo = 1 - x
+    tokens, width = grad_hbm.shape
+    tiles = w_hbm.shape[0] // TILE
+    rank = pin_hbm.shape[1]
+    own = rank // nmp
+    prow = tokens // PIECES
+    f32, bf16 = jnp.float32, jnp.bfloat16
+
+    def at(zz, xx):
+        return zz * COLS_X + xx
+
+    loads = [
+        pltpu.make_async_copy(src, dst, load_sem.at[i])
+        for i, (src, dst) in enumerate(
+            [
+                (grad_hbm, grad_v.at[me]), (x_hbm, x_v), (pin_hbm, pin_v), (pout_hbm, pout_v), (seq_hbm, seq_v),
+                (gate_hbm, gate_v), (up_hbm, up_v), (phid_hbm, phid_v), (pgate_hbm, pgate_v), (pup_hbm, pup_v),
+            ]
+        )
+    ]
+    for load in loads:
+        load.start()
+    w_loads = [
+        pltpu.make_async_copy(w_hbm.at[:, pl.ds(b * width, width)], w_v.at[b], w_sem.at[b]) for b in range(nmp)
+    ]
+    for load in w_loads:
+        load.start()
+
+    barrier = pltpu.get_barrier_semaphore()
+    mp_peers = [lax.rem(me + k, nmp) for k in range(1, nmp)]
+    dp_peers = [lax.rem(dp + k, ndp) for k in range(1, ndp)]
+    for peer in mp_peers:
+        pl.semaphore_signal(barrier, inc=1, device_id=(dp, peer), device_id_type=MESH)
+    for peer in dp_peers:
+        pl.semaphore_signal(barrier, inc=1, device_id=(peer, me), device_id_type=MESH)
+    loads[0].wait()
+    pl.semaphore_wait(barrier, len(mp_peers) + len(dp_peers))
+
+    def piece(kind, block, c, target):
+        ref = grad_v.at[block, pl.ds(pl.multiple_of(c * prow, prow), prow), :]
+        return pltpu.make_async_remote_copy(
+            src_ref=ref, dst_ref=ref, send_sem=g_send.at[kind, block, c], recv_sem=g_recv.at[block, c],
+            device_id=(dp, target), device_id_type=MESH,
+        )
+
+    def arrived(block, c):
+        piece(ACROSS, block, c, at(z, xo)).wait_recv()
+
+    def upward(block, c, op):
+        @pl.when(z < ROWS_Z - 1)
+        def _():
+            op(piece(UP, block, c, at(z + 1, x)))
+
+    def downward(block, c, op):
+        @pl.when(z > 0)
+        def _():
+            op(piece(DOWN, block, c, at(z - 1, x)))
+
+    def across(block, c, op):
+        op(piece(ACROSS, block, c, at(z, xo)))
+
+    def start(copy):
+        copy.start()
+
+    def done(copy):
+        copy.wait_send()
+
+    def own_block(op):
+        @pl.loop(0, PIECES)
+        def _(c):
+            across(me, c, op)
+            upward(me, c, op)
+            downward(me, c, op)
+
+    def same_column(level, op, wait):
+        @pl.loop(0, PIECES)
+        def _(c):
+            for sign, onward in ((1, downward), (-1, upward)):
+                far = z + sign * level
+
+                @pl.when((far >= 0) & (far < ROWS_Z))
+                def _():
+                    block = at(far, x)
+                    if wait:
+                        arrived(block, c)
+                    onward(block, c, op)
+                    if X_FIRST == 0:
+                        across(block, c, op)
+                    elif X_FIRST < PIECES:
+                        @pl.when(c >= X_FIRST)
+                        def _():
+                            across(block, c, op)
+
+    def crossed(dist, op, wait):
+        if X_FIRST == 0:
+            return
+
+        @pl.loop(0, X_FIRST)
+        def _(c):
+            if dist == 0:
+                block = at(z, xo)
+                if wait:
+                    arrived(block, c)
+                upward(block, c, op)
+                downward(block, c, op)
+                return
+            for sign, onward in ((1, downward), (-1, upward)):
+                far = z + sign * dist
+
+                @pl.when((far >= 0) & (far < ROWS_Z))
+                def _():
+                    block = at(far, xo)
+                    if wait:
+                        arrived(block, c)
+                    onward(block, c, op)
+
+    def rest_of(block):
+        @pl.loop(X_FIRST, PIECES)
+        def _(c):
+            arrived(block, c)
+
+    def add_block(block, first=False):
+        @pl.loop(0, tiles)
+        def _(n):
+            part = lax.dot_general(
+                grad_v[block], w_v[block, pl.ds(pl.multiple_of(n * TILE, TILE), TILE), :], NT,
+                preferred_element_type=f32,
+            )
+            if first:
+                hgrad[n] = part
+            else:
+                hgrad[n] += part
+
+    last_z = jnp.where(z < ROWS_Z // 2, ROWS_Z - 1, 0)
+    last = at(last_z, xo)
+
+    def add_level(level):
+        if level < ROWS_Z:
+            for sign in (1, -1):
+                far = z + sign * level
+
+                @pl.when((far >= 0) & (far < ROWS_Z))
+                def _():
+                    add_block(at(far, x))
+        for sign in (1, -1) if level > 1 else (1,):
+            far = z + sign * (level - 1)
+
+            @pl.when((far >= 0) & (far < ROWS_Z) & (far != last_z))
+            def _():
+                rest_of(at(far, xo))
+                add_block(at(far, xo))
+
+    own_block(start)
+
+    for load in loads[1:]:
+        load.wait()
+    out_t = lax.dot_general(pout_v[...], grad_v[me], NT, preferred_element_type=f32)
+    for p in range(nmp):
+        fac_send[p, 2 * own:3 * own, :] = out_t[p * own:(p + 1) * own, :]
+    acc_a[...] = jnp.dot(x_v[...], pin_v[...], preferred_element_type=f32)
+    acc_b[...] = jnp.zeros_like(acc_b)
+
+    @pl.loop(0, tiles)
+    def _(n):
+        cols = pl.ds(pl.multiple_of(n * TILE, TILE), TILE)
+
+        @pl.loop(0, tokens // ROWS)
+        def _(r):
+            rows = pl.ds(pl.multiple_of(r * ROWS, ROWS), ROWS)
+            g = gate_v[rows, cols].astype(f32)
+            u = up_v[rows, cols].astype(f32)
+            sig = 1.0 / (1.0 + jnp.exp(-g))
+            a = g * sig
+            act[n, rows, :] = a
+            upslope[n, rows, :] = u * (sig * (1.0 + g * (1.0 - sig)))
+            hid_tile[rows, :] = (a * u).astype(bf16)
+
+        acc_b[...] += jnp.dot(hid_tile[...], phid_v[cols, :], preferred_element_type=f32)
+
+    in_hid_t = jnp.concatenate([acc_a[...], acc_b[...]], axis=1).T
+    for p in range(nmp):
+        fac_send[p, 0:own, :] = in_hid_t[p * own:(p + 1) * own, :]
+        fac_send[p, own:2 * own, :] = in_hid_t[rank + p * own:rank + (p + 1) * own, :]
+
+    def exchange(src_of, dst, send_sems, recv_sems):
+        return [
+            pltpu.make_async_remote_copy(
+                src_ref=src_of(peer), dst_ref=dst.at[k], send_sem=send_sems.at[k], recv_sem=recv_sems.at[k],
+                device_id=(dp, peer), device_id_type=MESH,
+            )
+            for k, peer in enumerate(mp_peers)
+        ]
+
+    fac_copies = exchange(lambda peer: fac_send.at[peer], fac_recv, fac_ss, fac_rs)
+    for copy in fac_copies:
+        copy.start()
+
+    for load in w_loads:
+        load.wait()
+    add_block(me, first=True)
+
+    crossed(0, start, True)
+    same_column(1, start, True)
+    for copy in fac_copies:
+        copy.wait_recv()
+    mine = fac_send[me]
+    for k in range(nmp - 1):
+        mine = mine + fac_recv[k]
+    full[me] = jnp.concatenate([mine[0:own], mine[2 * own:3 * own]], axis=0).astype(bf16)
+    hid_own = mine[own:2 * own]
+    full_copies = [
+        pltpu.make_async_remote_copy(
+            src_ref=full.at[me], dst_ref=full.at[me], send_sem=full_ss.at[k], recv_sem=full_rs.at[k],
+            device_id=(dp, peer), device_id_type=MESH,
+        )
+        for k, peer in enumerate(mp_peers)
+    ]
+    for copy in full_copies:
+        copy.start()
+    add_level(1)
+
+    crossed(1, start, True)
+    same_column(2, start, True)
+    add_level(2)
+
+    crossed(2, start, True)
+    same_column(3, start, True)
+    add_level(3)
+
+    for copy in full_copies:
+        copy.wait_recv()
+    seqs = out_ref.shape[1]
+    member = (seq_v[...] == lax.broadcasted_iota(jnp.int32, (seqs, tokens), 0)).astype(f32)
+
+    @pl.loop(0, nmp)
+    def _(p):
+        block = full[p].astype(f32)
+        weighted[p] = jnp.concatenate([block[i:i + 1, :] * member for i in range(own)], axis=0).astype(bf16)
+
+    out_full = jnp.concatenate([full[p].astype(f32)[own:2 * own] for p in range(nmp)], axis=0)
+    weighted_hid = jnp.concatenate([hid_own[i:i + 1, :] * member for i in range(own)], axis=0)
+    hid_high = weighted_hid.astype(bf16)
+    hid_low = (weighted_hid - hid_high.astype(f32)).astype(bf16)
+    out_bf = out_full.astype(bf16)
+    raw_down = lax.dot_general(hid_high, out_bf, NT, preferred_element_type=f32) + lax.dot_general(
+        hid_low, out_bf, NT, preferred_element_type=f32
+    )
+    crossed(3, start, True)
+    rest_of(last)
+
+    acc_a[...] = jnp.zeros_like(acc_a)
+    acc_b[...] = jnp.zeros_like(acc_b)
+
+    @pl.loop(0, tiles)
+    def _(n):
+        cols = pl.ds(pl.multiple_of(n * TILE, TILE), TILE)
+        hgrad[n] += lax.dot_general(grad_v[last], w_v[last, cols, :], NT, preferred_element_type=f32)
+
+        @pl.loop(0, tokens // ROWS)
+        def _(r):
+            rows = pl.ds(pl.multiple_of(r * ROWS, ROWS), ROWS)
+            h = hgrad[n, rows, :]
+            hid_tile[rows, :] = (h * upslope[n, rows, :]).astype(bf16)
+            up_tile[rows, :] = (h * act[n, rows, :]).astype(bf16)
+
+        acc_a[...] += jnp.dot(hid_tile[...], pgate_v[cols, :], preferred_element_type=f32)
+        acc_b[...] += jnp.dot(up_tile[...], pup_v[cols, :], preferred_element_type=f32)
+
+    part = jnp.concatenate([acc_a[...], acc_b[...]], axis=1)
+    high = part.astype(bf16)
+    low = (part - high.astype(f32)).astype(bf16)
+
+    @pl.loop(0, nmp)
+    def _(p):
+        one = jnp.dot(weighted[p], high, preferred_element_type=f32) + jnp.dot(
+            weighted[p], low, preferred_element_type=f32
+        )
+        raw_own[p] = one
+        raw_send[p] = one.astype(bf16)
+
+    raw_copies = exchange(lambda peer: raw_send.at[peer], raw_recv, raw_ss, raw_rs)
+    for copy in raw_copies:
+        copy.start()
+    for copy in raw_copies:
+        copy.wait_recv()
+    raw = raw_own[me]
+    for k in range(nmp - 1):
+        raw = raw + raw_recv[k].astype(f32)
+
+    sq_pair = jnp.sum(raw * raw, axis=0, keepdims=True)
+    sq_down = jnp.sum(raw_down * raw_down, axis=0, keepdims=True)
+    sq_mine[...] = jnp.concatenate(
+        [sq_pair, jnp.concatenate([sq_down, jnp.zeros_like(sq_down)], axis=1), jnp.zeros((6, 2 * rank), f32)], axis=0
+    )
+    sq_copies = exchange(lambda peer: sq_mine, sq_recv, sq_ss, sq_rs)
+    for copy in sq_copies:
+        copy.start()
+    for copy in sq_copies:
+        copy.wait_recv()
+    total = sq_mine[...]
+    for k in range(nmp - 1):
+        total = total + sq_recv[k]
+    sq_group[...] = total
+    dp_copies = [
+        pltpu.make_async_remote_copy(
+            src_ref=sq_group, dst_ref=sq_dp.at[k], send_sem=dp_ss.at[k], recv_sem=dp_rs.at[k],
+            device_id=(peer, me), device_id_type=MESH,
+        )
+        for k, peer in enumerate(dp_peers)
+    ]
+    for copy in dp_copies:
+        copy.start()
+    for copy in dp_copies:
+        copy.wait_recv()
+    for k in range(ndp - 1):
+        total = total + sq_dp[k]
+    entries = seqs * ndp * rank * rank
+
+    def scale(values):
+        return lax.rsqrt(jnp.sum(values, axis=1, keepdims=True) / entries + 1e-06)
+
+    scale_gate = scale(total[0:1, :rank])
+    scale_up = scale(total[0:1, rank:])
+    scale_down = scale(total[1:2, :])
+    for q in range(own // 2):
+        lanes = slice(q * 2 * rank, (q + 1) * 2 * rank)
+        even = slice(2 * q * seqs, (2 * q + 1) * seqs)
+        odd = slice((2 * q + 1) * seqs, (2 * q + 2) * seqs)
+        out_ref[0, :, lanes] = jnp.concatenate([raw[even, :rank], raw[odd, :rank]], axis=1) * scale_gate
+        out_ref[1, :, lanes] = jnp.concatenate([raw[even, rank:], raw[odd, rank:]], axis=1) * scale_up
+        out_ref[2, :, lanes] = jnp.concatenate([raw_down[even], raw_down[odd]], axis=1) * scale_down
+
+    own_block(done)
+    for level in range(1, ROWS_Z):
+        same_column(level, done, False)
+    for dist in range(ROWS_Z):
+        crossed(dist, done, False)
+    for copy in fac_copies + full_copies + raw_copies + sq_copies + dp_copies:
+        copy.wait_send()
+
+
+def fused_device(ndp, nmp, *args):
+    layer_input, gate_pre, up_pre, out_grad, w_down, proj_input, _, _, _, proj_output, seq_ids = args
+    tokens, width = out_grad.shape
+    units = w_down.shape[0]
+    rank = proj_input.shape[1]
+    own = rank // nmp
+    tiles = units // TILE
+    f32, bf16 = jnp.float32, jnp.bfloat16
+    vmem, dma = pltpu.VMEM, pltpu.SemaphoreType.DMA
+    peers, dpeers = nmp - 1, max(ndp - 1, 1)
+    any_spec = pl.BlockSpec(memory_space=pl.ANY)
+    result = pl.pallas_call(
+        functools.partial(fused_kernel, ndp, nmp),
+        out_shape=jax.ShapeDtypeStruct((3, SEQ_DEV, own * rank), f32),
+        in_specs=[any_spec] * len(args),
+        out_specs=pl.BlockSpec(memory_space=pltpu.VMEM),
+        scratch_shapes=[
+            vmem(layer_input.shape, bf16),
+            vmem(gate_pre.shape, bf16),
+            vmem(up_pre.shape, bf16),
+            vmem((nmp, tokens, width), bf16),
+            vmem((nmp, units, width), bf16),
+            vmem(proj_input.shape, bf16),
+            vmem((units, rank), bf16),
+            vmem((units, rank), bf16),
+            vmem((units, rank), bf16),
+            vmem(proj_output.shape, bf16),
+            vmem(seq_ids.shape, jnp.int32),
+            vmem((tiles, tokens, TILE), f32),
+            vmem((tiles, tokens, TILE), f32),
+            vmem((tiles, tokens, TILE), f32),
+            vmem((tokens, TILE), bf16),
+            vmem((tokens, TILE), bf16),
+            vmem((tokens, rank), f32),
+            vmem((tokens, rank), f32),
+            vmem((nmp, 3 * own, tokens), f32),
+            vmem((peers, 3 * own, tokens), f32),
+            vmem((nmp, 2 * own, tokens), bf16),
+            vmem((nmp, own * SEQ_DEV, tokens), bf16),
+            vmem((nmp, own * SEQ_DEV, 2 * rank), f32),
+            vmem((nmp, own * SEQ_DEV, 2 * rank), bf16),
+            vmem((peers, own * SEQ_DEV, 2 * rank), bf16),
+            vmem((8, 2 * rank), f32),
+            vmem((peers, 8, 2 * rank), f32),
+            vmem((8, 2 * rank), f32),
+            vmem((dpeers, 8, 2 * rank), f32),
+            dma((10,)),
+            dma((nmp,)),
+            dma((3, nmp, PIECES)),
+            dma((nmp, PIECES)),
+            dma((peers,)), dma((peers,)),
+            dma((peers,)), dma((peers,)),
+            dma((peers,)), dma((peers,)),
+            dma((peers,)), dma((peers,)),
+            dma((dpeers,)), dma((dpeers,)),
+        ],
+        compiler_params=pltpu.CompilerParams(
+            collective_id=0, has_side_effects=True, vmem_limit_bytes=56 * 1024 * 1024
+        ),
+        cost_estimate=pl.CostEstimate(
+            flops=2 * tokens * units * width * nmp, bytes_accessed=2 * units * width * nmp,
+            transcendentals=tokens * units,
+        ),
+    )(*args)
+    return jnp.transpose(result, (1, 0, 2))
+
+
 def solution(mesh):
+    fits = mesh.shape["mp"] == ROWS_Z * COLS_X
+    body = functools.partial(fused_device, mesh.shape["dp"], mesh.shape["mp"]) if fits else per_device
     in_specs = (
         P("dp", "mp"),
         P("dp", "mp"),
@@ -103,5 +541,5 @@
     )
     out_specs = P("dp", None, "mp")
     return jax.shard_map(
-        per_device, mesh=mesh, in_specs=in_specs, out_specs=out_specs, check_vma=False
-    )
+        body, mesh=mesh, in_specs=in_specs, out_specs=out_specs, check_vma=False
+    )

time: 229 us -> 90.2 us (0.39)
  waiting for transfers between devices: 147 us -> 0 us
  Pallas kernels: 0 us -> 81.1 us
  blocking collectives: 39.4 us -> 0 us
  matrix products: 25.5 us -> 0 us
  between operations: 13.5 us -> 0.01 us
  local copies, waits for them, and re-layouts: 1.28 us -> 8.79 us
    pallas_call x0 -> x1, Pallas kernels: none -> 81.1 us  [fused_device(): pl.pallas_call(functools.partial(fused_kernel, ndp, nmp), out_shape=jax.S...]
    psum x1 -> x0, waiting for transfers between devices: 74 us -> none  [per_device(): lax.psum((in_part, hid_part, gate_part, up_part, out_part), 'mp')]
    all_gather x1 -> x0, waiting for transfers between devices: 71.8 us -> none  [per_device(): lax.all_gather(out_grad, 'mp', axis=1, tiled=True)]
    psum x1 -> x0, blocking collectives: 39.4 us -> none  [per_device(): total_sq = lax.psum(squares, ('dp', 'mp'))]
    dot_general x8 -> x0, matrix products: 25.5 us -> none  [the longest x1 11.9 us: per_device(): lax.dot_general(lax.all_gather(out_grad, 'mp', axis=1, tiled=True), w_dow...]
    unnamed x14 -> x5, local copies, waits for them, and re-layouts: 0.3 us -> 8.79 us
  transfers between devices with their start and end apart: 2 -> 0, of which waited for: 2 -> 0; matrix products, arithmetic and copies ran while one was open for 3% -> 0% of each run, Pallas kernels for 0% -> 0%
where the time goes in v1:
time: 90.2 us; the launch traced here: 89.9 us
  Pallas kernels  81.1 us (90%)
  local copies, waits for them, and re-layouts  8.79 us (10%)
    pallas_call x1, Pallas kernels, fused_device(): pl.pallas_call(functools.partial(fused_kernel, ndp, nmp), out_shape=jax.S...  81.1 us
    unnamed x5, local copies, waits for them, and re-layouts  8.79 us

profile of v1, /device:TPU:0, one launch (start us, length us, event | category | flops | bytes accessed | tf_op | source)
XLA Modules:
  0.0 89.9 jit_solution(6028925859544118576)
XLA Ops:
  0.0 1.6 %copy.12.pin_hbm = bf16[512,64]{1,0:T(8,128)(2,1)} copy(bf16[512,64]{0,1:T(8,128)(2,1)} %param.16) | data formatting | bytes 131072 | tf_op args[5]
  1.6 1.9 %copy.13.phid_hbm = bf16[1792,64]{1,0:T(8,128)(2,1)} copy(bf16[1792,64]{0,1:T(8,128)(2,1)} %param.17) | data formatting | bytes 458752 | tf_op args[6]
  3.5 1.9 %copy.14.pgate_hbm = bf16[1792,64]{1,0:T(8,128)(2,1)} copy(bf16[1792,64]{0,1:T(8,128)(2,1)} %param.18) | data formatting | bytes 458752 | tf_op args[7]
  5.4 1.9 %copy.15.pup_hbm = bf16[1792,64]{1,0:T(8,128)(2,1)} copy(bf16[1792,64]{0,1:T(8,128)(2,1)} %param.19) | data formatting | bytes 458752 | tf_op args[8]
  7.4 81.1 %shard_map.109 = f32[3,8,512]{2,1,0:T(8,128)} custom-call(bf16[512,512]{1,0:T(8,128)(2,1)} %x_hbm.1, bf16[512,1792]{1,0:T(8,128)(2,1)} %gate_hbm.1, bf16[512,1792]{1,0:T(8,128)(2,1)} %up_hbm.1, bf16[512,512]{1,0:T(8,128)(2,1)} %grad_hbm.1, bf16[1792,4096]{1,0:T(8,128)(2,1)} %w_hbm.1, bf16[512,64]{1,0:T(8,128)(2,1)} %copy.12.pin_hbm, ...), custom_call_target="tpu_custom_call" | custom-call | flops 7516192768 | bytes 14680064 | tf_op jit(solution)/shard_map/pallas_call | solution.py:470
  88.5 1.4 %copy.17 = f32[8,3,512]{2,0,1:T(8,128)} copy(f32[8,3,512]{2,0,1:T(8,128)} %bitcast.1) | data formatting | bytes 98304

commit v2 on v1

--- a/solution.py
+++ b/solution.py
@@ -93,8 +93,8 @@
 
 MESH = pl.DeviceIdType.MESH
 ROWS_Z, COLS_X = 4, 2
-PIECES = 4
-X_FIRST = 0
+PIECES = 8
+X_FIRST = 1
 TILE = 256
 ROWS = 128
 NT = (((1,), (1,)), ((), ()))
@@ -106,7 +106,7 @@
     x_hbm, gate_hbm, up_hbm, grad_hbm, w_hbm, pin_hbm, phid_hbm, pgate_hbm, pup_hbm, pout_hbm, seq_hbm,
     out_ref,
     x_v, gate_v, up_v, grad_v, w_v, pin_v, phid_v, pgate_v, pup_v, pout_v, seq_v,
-    hgrad, act, upslope, hid_tile, up_tile, acc_a, acc_b,
+    hgrad, act, upslope, hid_tile, up_tile, acc_hid, acc_a, acc_b,
     fac_send, fac_recv, full, weighted, raw_own, raw_send, raw_recv,
     sq_mine, sq_recv, sq_group, sq_dp,
     load_sem, w_sem, g_send, g_recv, fac_ss, fac_rs, full_ss, full_rs, raw_ss, raw_rs,
@@ -118,7 +118,7 @@
     xo = 1 - x
     tokens, width = grad_hbm.shape
     tiles = w_hbm.shape[0] // TILE
-    rank = pin_hbm.shape[1]
+    rank = pin_hbm.shape[0]
     own = rank // nmp
     prow = tokens // PIECES
     f32, bf16 = jnp.float32, jnp.bfloat16
@@ -153,91 +153,93 @@
     loads[0].wait()
     pl.semaphore_wait(barrier, len(mp_peers) + len(dp_peers))
 
-    def piece(kind, block, c, target):
-        ref = grad_v.at[block, pl.ds(pl.multiple_of(c * prow, prow), prow), :]
+    def rows_of(kind, block, start, count, target):
+        ref = grad_v.at[block, pl.ds(start, count), :]
         return pltpu.make_async_remote_copy(
-            src_ref=ref, dst_ref=ref, send_sem=g_send.at[kind, block, c], recv_sem=g_recv.at[block, c],
+            src_ref=ref, dst_ref=ref, send_sem=g_send.at[kind, block], recv_sem=g_recv.at[block, start // prow],
             device_id=(dp, target), device_id_type=MESH,
         )
 
+    def piece(kind, block, c, target):
+        return rows_of(kind, block, pl.multiple_of(c * prow, prow), prow, target)
+
     def arrived(block, c):
         piece(ACROSS, block, c, at(z, xo)).wait_recv()
 
-    def upward(block, c, op):
+    def upward(block, c):
         @pl.when(z < ROWS_Z - 1)
         def _():
-            op(piece(UP, block, c, at(z + 1, x)))
-
-    def downward(block, c, op):
+            piece(UP, block, c, at(z + 1, x)).start()
+
+    def downward(block, c):
         @pl.when(z > 0)
         def _():
-            op(piece(DOWN, block, c, at(z - 1, x)))
-
-    def across(block, c, op):
-        op(piece(ACROSS, block, c, at(z, xo)))
-
-    def start(copy):
-        copy.start()
-
-    def done(copy):
-        copy.wait_send()
-
-    def own_block(op):
-        @pl.loop(0, PIECES)
-        def _(c):
-            across(me, c, op)
-            upward(me, c, op)
-            downward(me, c, op)
-
-    def same_column(level, op, wait):
-        @pl.loop(0, PIECES)
-        def _(c):
-            for sign, onward in ((1, downward), (-1, upward)):
-                far = z + sign * level
-
-                @pl.when((far >= 0) & (far < ROWS_Z))
+            piece(DOWN, block, c, at(z - 1, x)).start()
+
+    def across(block, c):
+        piece(ACROSS, block, c, at(z, xo)).start()
+
+    def inside(far):
+        return (far >= 0) & (far < ROWS_Z)
+
+    def pass_on(level, c):
+        for sign, onward in ((1, downward), (-1, upward)):
+            far = z + sign * level
+
+            @pl.when(inside(far))
+            def _():
+                arrived(at(far, x), c)
+                onward(at(far, x), c)
+
+                @pl.when(c >= X_FIRST)
                 def _():
-                    block = at(far, x)
-                    if wait:
-                        arrived(block, c)
-                    onward(block, c, op)
-                    if X_FIRST == 0:
-                        across(block, c, op)
-                    elif X_FIRST < PIECES:
-                        @pl.when(c >= X_FIRST)
-                        def _():
-                            across(block, c, op)
-
-    def crossed(dist, op, wait):
-        if X_FIRST == 0:
-            return
-
-        @pl.loop(0, X_FIRST)
-        def _(c):
-            if dist == 0:
+                    across(at(far, x), c)
+
+        @pl.when(c < X_FIRST)
+        def _():
+            if level == 1:
                 block = at(z, xo)
-                if wait:
-                    arrived(block, c)
-                upward(block, c, op)
-                downward(block, c, op)
+                arrived(block, c)
+                upward(block, c)
+                downward(block, c)
                 return
             for sign, onward in ((1, downward), (-1, upward)):
-                far = z + sign * dist
-
-                @pl.when((far >= 0) & (far < ROWS_Z))
+                far = z + sign * (level - 1)
+
+                @pl.when(inside(far))
                 def _():
-                    block = at(far, xo)
-                    if wait:
-                        arrived(block, c)
-                    onward(block, c, op)
+                    arrived(at(far, xo), c)
+                    onward(at(far, xo), c)
+
+    def sent(kind, block, start, stop):
+        if stop > start:
+            target = {UP: at(z + 1, x), DOWN: at(z - 1, x), ACROSS: at(z, xo)}[kind]
+            rows_of(kind, block, start * prow, (stop - start) * prow, target).wait_send()
+
+    def all_sent(dist):
+        for sign, kind in ((1, DOWN), (-1, UP)):
+            far = z + sign * dist
+            goes = z > 0 if kind == DOWN else z < ROWS_Z - 1
+
+            @pl.when(inside(far) & goes)
+            def _():
+                sent(kind, at(far, x), 0, PIECES)
+                sent(kind, at(far, xo), 0, X_FIRST)
+
+            if dist > 0:
+                @pl.when(inside(far))
+                def _():
+                    sent(ACROSS, at(far, x), X_FIRST, PIECES)
+        if dist == 0:
+            sent(ACROSS, me, 0, PIECES)
 
     def rest_of(block):
         @pl.loop(X_FIRST, PIECES)
         def _(c):
             arrived(block, c)
 
-    def add_block(block, first=False):
-        @pl.loop(0, tiles)
+    def add_block(block, low, high, first=False):
+        @pl.loop(low, high)
         def _(n):
             part = lax.dot_general(
                 grad_v[block], w_v[block, pl.ds(pl.multiple_of(n * TILE, TILE), TILE), :], NT,
@@ -248,34 +250,49 @@
             else:
                 hgrad[n] += part
 
+    def share(c):
+        return c * tiles // PIECES, (c + 1) * tiles // PIECES
+
     last_z = jnp.where(z < ROWS_Z // 2, ROWS_Z - 1, 0)
     last = at(last_z, xo)
 
-    def add_level(level):
+    def level_blocks(level, op_near, op_far):
         if level < ROWS_Z:
             for sign in (1, -1):
                 far = z + sign * level
 
-                @pl.when((far >= 0) & (far < ROWS_Z))
+                @pl.when(inside(far))
                 def _():
-                    add_block(at(far, x))
+                    op_near(at(far, x))
         for sign in (1, -1) if level > 1 else (1,):
-            far = z + sign * (level - 1)
-
-            @pl.when((far >= 0) & (far < ROWS_Z) & (far != last_z))
+            far2 = z + sign * (level - 1)
+
+            @pl.when(inside(far2) & (far2 != last_z))
             def _():
-                rest_of(at(far, xo))
-                add_block(at(far, xo))
-
-    own_block(start)
+                op_far(at(far2, xo))
+
+    def await_level(level):
+        level_blocks(level, lambda block: None, rest_of)
+
+    def add_level(level, low, high):
+        add = lambda block: add_block(block, low, high)
+        level_blocks(level, add, add)
+
+    @pl.loop(0, PIECES)
+    def _(c):
+        across(me, c)
+        upward(me, c)
+        downward(me, c)
 
     for load in loads[1:]:
         load.wait()
     out_t = lax.dot_general(pout_v[...], grad_v[me], NT, preferred_element_type=f32)
     for p in range(nmp):
         fac_send[p, 2 * own:3 * own, :] = out_t[p * own:(p + 1) * own, :]
-    acc_a[...] = jnp.dot(x_v[...], pin_v[...], preferred_element_type=f32)
-    acc_b[...] = jnp.zeros_like(acc_b)
+    in_t = lax.dot_general(pin_v[...], x_v[...], NT, preferred_element_type=f32)
+    for p in range(nmp):
+        fac_send[p, 0:own, :] = in_t[p * own:(p + 1) * own, :]
+    acc_hid[...] = jnp.zeros_like(acc_hid)
 
     @pl.loop(0, tiles)
     def _(n):
@@ -292,12 +309,10 @@
             upslope[n, rows, :] = u * (sig * (1.0 + g * (1.0 - sig)))
             hid_tile[rows, :] = (a * u).astype(bf16)
 
-        acc_b[...] += jnp.dot(hid_tile[...], phid_v[cols, :], preferred_element_type=f32)
-
-    in_hid_t = jnp.concatenate([acc_a[...], acc_b[...]], axis=1).T
+        acc_hid[...] += lax.dot_general(phid_v[:, cols], hid_tile[...], NT, preferred_element_type=f32)
+
     for p in range(nmp):
-        fac_send[p, 0:own, :] = in_hid_t[p * own:(p + 1) * own, :]
-        fac_send[p, own:2 * own, :] = in_hid_t[rank + p * own:rank + (p + 1) * own, :]
+        fac_send[p, own:2 * own, :] = acc_hid[p * own:(p + 1) * own, :]
 
     def exchange(src_of, dst, send_sems, recv_sems):
         return [
@@ -314,10 +329,19 @@
 
     for load in w_loads:
         load.wait()
-    add_block(me, first=True)
-
-    crossed(0, start, True)
-    same_column(1, start, True)
+
+    @pl.loop(0, PIECES)
+    def _(c):
+        pass_on(1, c)
+        add_block(me, *share(c), first=True)
+
+    await_level(1)
+
+    @pl.loop(0, PIECES)
+    def _(c):
+        pass_on(2, c)
+        add_level(1, *share(c))
+
     for copy in fac_copies:
         copy.wait_recv()
     mine = fac_send[me]
@@ -334,15 +358,15 @@
     ]
     for copy in full_copies:
         copy.start()
-    add_level(1)
-
-    crossed(1, start, True)
-    same_column(2, start, True)
-    add_level(2)
-
-    crossed(2, start, True)
-    same_column(3, start, True)
-    add_level(3)
+    await_level(2)
+
+    @pl.loop(0, PIECES)
+    def _(c):
+        pass_on(3, c)
+        add_level(2, *share(c))
+
+    await_level(3)
+    add_level(3, 0, tiles)
 
     for copy in full_copies:
         copy.wait_recv()
@@ -362,26 +386,40 @@
     raw_down = lax.dot_general(hid_high, out_bf, NT, preferred_element_type=f32) + lax.dot_general(
         hid_low, out_bf, NT, preferred_element_type=f32
     )
-    crossed(3, start, True)
-    rest_of(last)
+    all_sent(0)
+    all_sent(1)
 
     acc_a[...] = jnp.zeros_like(acc_a)
     acc_b[...] = jnp.zeros_like(acc_b)
 
-    @pl.loop(0, tiles)
-    def _(n):
-        cols = pl.ds(pl.multiple_of(n * TILE, TILE), TILE)
-        hgrad[n] += lax.dot_general(grad_v[last], w_v[last, cols, :], NT, preferred_element_type=f32)
-
-        @pl.loop(0, tokens // ROWS)
-        def _(r):
-            rows = pl.ds(pl.multiple_of(r * ROWS, ROWS), ROWS)
-            h = hgrad[n, rows, :]
-            hid_tile[rows, :] = (h * upslope[n, rows, :]).astype(bf16)
-            up_tile[rows, :] = (h * act[n, rows, :]).astype(bf16)
-
-        acc_a[...] += jnp.dot(hid_tile[...], pgate_v[cols, :], preferred_element_type=f32)
-        acc_b[...] += jnp.dot(up_tile[...], pup_v[cols, :], preferred_element_type=f32)
+    half = tokens // 2
+    for part_no in range(2):
+        at_end = (z == 0) | (z == ROWS_Z - 1)
+        for c in range(part_no * PIECES // 2, (part_no + 1) * PIECES // 2):
+            if c < X_FIRST:
+                @pl.when(at_end)
+                def _():
+                    arrived(last, c)
+            else:
+                arrived(last, c)
+        span = slice(part_no * half, (part_no + 1) * half)
+
+        @pl.loop(0, tiles)
+        def _(n):
+            cols = pl.ds(pl.multiple_of(n * TILE, TILE), TILE)
+            hgrad[n, span, :] += lax.dot_general(
+                grad_v[last, span, :], w_v[last, cols, :], NT, preferred_element_type=f32
+            )
+
+            @pl.loop(part_no * half // ROWS, (part_no + 1) * half // ROWS)
+            def _(r):
+                rows = pl.ds(pl.multiple_of(r * ROWS, ROWS), ROWS)
+                h = hgrad[n, rows, :]
+                hid_tile[rows, :] = (h * upslope[n, rows, :]).astype(bf16)
+                up_tile[rows, :] = (h * act[n, rows, :]).astype(bf16)
+
+            acc_a[span, :] += lax.dot_general(hid_tile[span, :], pgate_v[:, cols], NT, preferred_element_type=f32)
+            acc_b[span, :] += lax.dot_general(up_tile[span, :], pup_v[:, cols], NT, preferred_element_type=f32)
 
     part = jnp.concatenate([acc_a[...], acc_b[...]], axis=1)
     high = part.astype(bf16)
@@ -398,6 +436,10 @@
     raw_copies = exchange(lambda peer: raw_send.at[peer], raw_recv, raw_ss, raw_rs)
     for copy in raw_copies:
         copy.start()
+    all_sent(2)
+    all_sent(3)
+    for copy in fac_copies + full_copies:
+        copy.wait_send()
     for copy in raw_copies:
         copy.wait_recv()
     raw = raw_own[me]
@@ -447,20 +489,16 @@
         out_ref[1, :, lanes] = jnp.concatenate([raw[even, rank:], raw[odd, rank:]], axis=1) * scale_up
         out_ref[2, :, lanes] = jnp.concatenate([raw_down[even], raw_down[odd]], axis=1) * scale_down
 
-    own_block(done)
-    for level in range(1, ROWS_Z):
-        same_column(level, done, False)
-    for dist in range(ROWS_Z):
-        crossed(dist, done, False)
-    for copy in fac_copies + full_copies + raw_copies + sq_copies + dp_copies:
+    for copy in raw_copies + sq_copies + dp_copies:
         copy.wait_send()
 
 
 def fused_device(ndp, nmp, *args):
-    layer_input, gate_pre, up_pre, out_grad, w_down, proj_input, _, _, _, proj_output, seq_ids = args
+    layer_input, gate_pre, up_pre, out_grad, w_down, *projections, proj_output, seq_ids = args
     tokens, width = out_grad.shape
     units = w_down.shape[0]
-    rank = proj_input.shape[1]
+    proj_input, proj_hidden, proj_gate, proj_upward = [proj.T for proj in projections]
+    rank = proj_output.shape[0]
     own = rank // nmp
     tiles = units // TILE
     f32, bf16 = jnp.float32, jnp.bfloat16
@@ -479,9 +517,9 @@
             vmem((nmp, tokens, width), bf16),
             vmem((nmp, units, width), bf16),
             vmem(proj_input.shape, bf16),
-            vmem((units, rank), bf16),
-            vmem((units, rank), bf16),
-            vmem((units, rank), bf16),
+            vmem((rank, units), bf16),
+            vmem((rank, units), bf16),
+            vmem((rank, units), bf16),
             vmem(proj_output.shape, bf16),
             vmem(seq_ids.shape, jnp.int32),
             vmem((tiles, tokens, TILE), f32),
@@ -489,6 +527,7 @@
             vmem((tiles, tokens, TILE), f32),
             vmem((tokens, TILE), bf16),
             vmem((tokens, TILE), bf16),
+            vmem((rank, tokens), f32),
             vmem((tokens, rank), f32),
             vmem((tokens, rank), f32),
             vmem((nmp, 3 * own, tokens), f32),
@@ -504,7 +543,7 @@
             vmem((dpeers, 8, 2 * rank), f32),
             dma((10,)),
             dma((nmp,)),
-            dma((3, nmp, PIECES)),
+            dma((3, nmp)),
             dma((nmp, PIECES)),
             dma((peers,)), dma((peers,)),
             dma((peers,)), dma((peers,)),
@@ -519,7 +558,10 @@
             flops=2 * tokens * units * width * nmp, bytes_accessed=2 * units * width * nmp,
             transcendentals=tokens * units,
         ),
-    )(*args)
+    )(
+        layer_input, gate_pre, up_pre, out_grad, w_down, proj_input, proj_hidden, proj_gate, proj_upward, proj_output,
+        seq_ids,
+    )
     return jnp.transpose(result, (1, 0, 2))
 
 

time: 90.2 us -> 84.4 us (0.936)
  local copies, waits for them, and re-layouts: 8.79 us -> 1.42 us
  Pallas kernels: 81.1 us -> 82.8 us
    unnamed x5 -> x1, local copies, waits for them, and re-layouts: 8.79 us -> 1.42 us
    pallas_call x1, Pallas kernels: 81.1 us -> 82.8 us  [fused_device(): pl.pallas_call(functools.partial(fused_kernel, ndp, nmp), out_shape=jax.S...]
where the time goes in v2:
time: 84.4 us; the launch traced here: 84.3 us
  Pallas kernels  82.8 us (98%)
  local copies, waits for them, and re-layouts  1.42 us (2%)
    pallas_call x1, Pallas kernels, fused_device(): pl.pallas_call(functools.partial(fused_kernel, ndp, nmp), out_shape=jax.S...  82.8 us

profile of v2, /device:TPU:0, one launch (start us, length us, event | category | flops | bytes accessed | tf_op | source)
XLA Modules:
  0.0 84.3 jit_solution(15990460100850991340)
XLA Ops:
  0.0 82.8 %shard_map.109 = f32[3,8,512]{2,1,0:T(8,128)} custom-call(bf16[512,512]{1,0:T(8,128)(2,1)} %x_hbm.1, bf16[512,1792]{1,0:T(8,128)(2,1)} %gate_hbm.1, bf16[512,1792]{1,0:T(8,128)(2,1)} %up_hbm.1, bf16[512,512]{1,0:T(8,128)(2,1)} %grad_hbm.1, bf16[1792,4096]{1,0:T(8,128)(2,1)} %w_hbm.1, bf16[64,512]{1,0:T(8,128)(2,1)} %bitcast.9, bf16[64,1792]{1,0:T(8,128)(2,1)} %bitcast.6, ...), custom_call_target="tpu_custom_call" | custom-call | flops 7516192768 | bytes 14680064 | tf_op jit(solution)/shard_map/pallas_call | solution.py:508
  82.8 1.4 %copy.13 = f32[8,3,512]{2,0,1:T(8,128)} copy(f32[8,3,512]{2,0,1:T(8,128)} %bitcast.5) | data formatting | bytes 98304

commit v3 on v2

--- a/solution.py
+++ b/solution.py
@@ -106,7 +106,7 @@
     x_hbm, gate_hbm, up_hbm, grad_hbm, w_hbm, pin_hbm, phid_hbm, pgate_hbm, pup_hbm, pout_hbm, seq_hbm,
     out_ref,
     x_v, gate_v, up_v, grad_v, w_v, pin_v, phid_v, pgate_v, pup_v, pout_v, seq_v,
-    hgrad, act, upslope, hid_tile, up_tile, acc_hid, acc_a, acc_b,
+    grad_t, hgrad, act, upslope, hid_tile, up_tile, acc_hid, acc_a, acc_b,
     fac_send, fac_recv, full, weighted, raw_own, raw_send, raw_recv,
     sq_mine, sq_recv, sq_group, sq_dp,
     load_sem, w_sem, g_send, g_recv, fac_ss, fac_rs, full_ss, full_rs, raw_ss, raw_rs,
@@ -238,13 +238,17 @@
         def _(c):
             arrived(block, c)
 
+    def turn(block, low=0, high=tokens // ROWS):
+        @pl.loop(low, high)
+        def _(r):
+            rows = pl.ds(pl.multiple_of(r * ROWS, ROWS), ROWS)
+            grad_t[block, :, rows] = grad_v[block, rows, :].T
+
     def add_block(block, low, high, first=False):
         @pl.loop(low, high)
         def _(n):
-            part = lax.dot_general(
-                grad_v[block], w_v[block, pl.ds(pl.multiple_of(n * TILE, TILE), TILE), :], NT,
-                preferred_element_type=f32,
-            )
+            units = pl.ds(pl.multiple_of(n * TILE, TILE), TILE)
+            part = jnp.dot(w_v[block, units, :], grad_t[block], preferred_element_type=f32)
             if first:
                 hgrad[n] = part
             else:
@@ -272,7 +276,11 @@
                 op_far(at(far2, xo))
 
     def await_level(level):
-        level_blocks(level, lambda block: None, rest_of)
+        def whole(block):
+            rest_of(block)
+            turn(block)
+
+        level_blocks(level, turn, whole)
 
     def add_level(level, low, high):
         add = lambda block: add_block(block, low, high)
@@ -286,7 +294,8 @@
 
     for load in loads[1:]:
         load.wait()
-    out_t = lax.dot_general(pout_v[...], grad_v[me], NT, preferred_element_type=f32)
+    turn(me)
+    out_t = jnp.dot(pout_v[...], grad_t[me], preferred_element_type=f32)
     for p in range(nmp):
         fac_send[p, 2 * own:3 * own, :] = out_t[p * own:(p + 1) * own, :]
     in_t = lax.dot_general(pin_v[...], x_v[...], NT, preferred_element_type=f32)
@@ -301,15 +310,15 @@
         @pl.loop(0, tokens // ROWS)
         def _(r):
             rows = pl.ds(pl.multiple_of(r * ROWS, ROWS), ROWS)
-            g = gate_v[rows, cols].astype(f32)
-            u = up_v[rows, cols].astype(f32)
+            g = gate_v[rows, cols].T.astype(f32)
+            u = up_v[rows, cols].T.astype(f32)
             sig = 1.0 / (1.0 + jnp.exp(-g))
             a = g * sig
-            act[n, rows, :] = a
-            upslope[n, rows, :] = u * (sig * (1.0 + g * (1.0 - sig)))
-            hid_tile[rows, :] = (a * u).astype(bf16)
-
-        acc_hid[...] += lax.dot_general(phid_v[:, cols], hid_tile[...], NT, preferred_element_type=f32)
+            act[n, :, rows] = a
+            upslope[n, :, rows] = u * (sig * (1.0 + g * (1.0 - sig)))
+            hid_tile[:, rows] = (a * u).astype(bf16)
+
+        acc_hid[...] += jnp.dot(phid_v[:, cols], hid_tile[...], preferred_element_type=f32)
 
     for p in range(nmp):
         fac_send[p, own:2 * own, :] = acc_hid[p * own:(p + 1) * own, :]
@@ -403,25 +412,24 @@
             else:
                 arrived(last, c)
         span = slice(part_no * half, (part_no + 1) * half)
+        turn(last, part_no * half // ROWS, (part_no + 1) * half // ROWS)
 
         @pl.loop(0, tiles)
         def _(n):
             cols = pl.ds(pl.multiple_of(n * TILE, TILE), TILE)
-            hgrad[n, span, :] += lax.dot_general(
-                grad_v[last, span, :], w_v[last, cols, :], NT, preferred_element_type=f32
-            )
+            hgrad[n, :, span] += jnp.dot(w_v[last, cols, :], grad_t[last, :, span], preferred_element_type=f32)
 
             @pl.loop(part_no * half // ROWS, (part_no + 1) * half // ROWS)
             def _(r):
                 rows = pl.ds(pl.multiple_of(r * ROWS, ROWS), ROWS)
-                h = hgrad[n, rows, :]
-                hid_tile[rows, :] = (h * upslope[n, rows, :]).astype(bf16)
-                up_tile[rows, :] = (h * act[n, rows, :]).astype(bf16)
-
-            acc_a[span, :] += lax.dot_general(hid_tile[span, :], pgate_v[:, cols], NT, preferred_element_type=f32)
-            acc_b[span, :] += lax.dot_general(up_tile[span, :], pup_v[:, cols], NT, preferred_element_type=f32)
-
-    part = jnp.concatenate([acc_a[...], acc_b[...]], axis=1)
+                h = hgrad[n, :, rows]
+                hid_tile[:, rows] = (h * upslope[n, :, rows]).astype(bf16)
+                up_tile[:, rows] = (h * act[n, :, rows]).astype(bf16)
+
+            acc_a[:, span] += jnp.dot(pgate_v[:, cols], hid_tile[:, span], preferred_element_type=f32)
+            acc_b[:, span] += jnp.dot(pup_v[:, cols], up_tile[:, span], preferred_element_type=f32)
+
+    part = jnp.concatenate([acc_a[...], acc_b[...]], axis=0).T
     high = part.astype(bf16)
     low = (part - high.astype(f32)).astype(bf16)
 
@@ -522,14 +530,15 @@
             vmem((rank, units), bf16),
             vmem(proj_output.shape, bf16),
             vmem(seq_ids.shape, jnp.int32),
-            vmem((tiles, tokens, TILE), f32),
-            vmem((tiles, tokens, TILE), f32),
-            vmem((tiles, tokens, TILE), f32),
-            vmem((tokens, TILE), bf16),
-            vmem((tokens, TILE), bf16),
+            vmem((nmp, width, tokens), bf16),
+            vmem((tiles, TILE, tokens), f32),
+            vmem((tiles, TILE, tokens), f32),
+            vmem((tiles, TILE, tokens), f32),
+            vmem((TILE, tokens), bf16),
+            vmem((TILE, tokens), bf16),
             vmem((rank, tokens), f32),
-            vmem((tokens, rank), f32),
-            vmem((tokens, rank), f32),
+            vmem((rank, tokens), f32),
+            vmem((rank, tokens), f32),
             vmem((nmp, 3 * own, tokens), f32),
             vmem((peers, 3 * own, tokens), f32),
             vmem((nmp, 2 * own, tokens), bf16),

time: 84.4 us -> 84.4 us (level)
  no operation moved by 1% of the time
where the time goes in v3:
time: 84.4 us; the launch traced here: 84.2 us
  Pallas kernels  82.8 us (98%)
  local copies, waits for them, and re-layouts  1.42 us (2%)
    pallas_call x1, Pallas kernels, fused_device(): pl.pallas_call(functools.partial(fused_kernel, ndp, nmp), out_shape=jax.S...  82.8 us

profile of v3, /device:TPU:0, one launch (start us, length us, event | category | flops | bytes accessed | tf_op | source)
XLA Modules:
  0.0 84.2 jit_solution(6553749831658258625)
XLA Ops:
  0.0 82.8 %shard_map.109 = f32[3,8,512]{2,1,0:T(8,128)} custom-call(bf16[512,512]{1,0:T(8,128)(2,1)} %x_hbm.1, bf16[512,1792]{1,0:T(8,128)(2,1)} %gate_hbm.1, bf16[512,1792]{1,0:T(8,128)(2,1)} %up_hbm.1, bf16[512,512]{1,0:T(8,128)(2,1)} %grad_hbm.1, bf16[1792,4096]{1,0:T(8,128)(2,1)} %w_hbm.1, bf16[64,512]{1,0:T(8,128)(2,1)} %bitcast.9, bf16[64,1792]{1,0:T(8,128)(2,1)} %bitcast.6, ...), custom_call_target="tpu_custom_call" | custom-call | flops 7516192768 | bytes 14680064 | tf_op jit(solution)/shard_map/pallas_call | solution.py:516
  82.8 1.4 %copy.13 = f32[8,3,512]{2,0,1:T(8,128)} copy(f32[8,3,512]{2,0,1:T(8,128)} %bitcast.5) | data formatting | bytes 98304

commit v4 on v3

--- a/solution.py
+++ b/solution.py
@@ -93,12 +93,11 @@
 
 MESH = pl.DeviceIdType.MESH
 ROWS_Z, COLS_X = 4, 2
-PIECES = 8
-X_FIRST = 1
+PIECES = 4
 TILE = 256
 ROWS = 128
 NT = (((1,), (1,)), ((), ()))
-UP, DOWN, ACROSS = 0, 1, 2
+ACROSS = ROWS_Z
 
 
 def fused_kernel(
@@ -166,75 +165,71 @@
     def arrived(block, c):
         piece(ACROSS, block, c, at(z, xo)).wait_recv()
 
-    def upward(block, c):
-        @pl.when(z < ROWS_Z - 1)
-        def _():
-            piece(UP, block, c, at(z + 1, x)).start()
-
-    def downward(block, c):
-        @pl.when(z > 0)
-        def _():
-            piece(DOWN, block, c, at(z - 1, x)).start()
-
     def across(block, c):
         piece(ACROSS, block, c, at(z, xo)).start()
 
+    def along(block, c, target_z):
+        piece(target_z, block, c, at(target_z, x)).start()
+
     def inside(far):
         return (far >= 0) & (far < ROWS_Z)
 
+    at_end = (z == 0) | (z == ROWS_Z - 1)
+
+    def own_targets(op):
+        for dist in range(ROWS_Z - 1, 0, -1):
+            for sign in (1, -1):
+                target_z = z + sign * dist
+                goes = inside(target_z)
+
+                @pl.when(goes if dist == 1 else goes & at_end)
+                def _():
+                    op(target_z)
+
+    def handed_on(op):
+        for sign in (1, -1):
+            far, target_z = z + sign, z - sign
+
+            @pl.when(inside(far) & (far != 0) & (far != ROWS_Z - 1) & jnp.logical_not(at_end))
+            def _():
+                op(at(far, x), target_z)
+
     def pass_on(level, c):
-        for sign, onward in ((1, downward), (-1, upward)):
+        for sign in (1, -1):
             far = z + sign * level
 
             @pl.when(inside(far))
             def _():
                 arrived(at(far, x), c)
-                onward(at(far, x), c)
-
-                @pl.when(c >= X_FIRST)
-                def _():
-                    across(at(far, x), c)
-
-        @pl.when(c < X_FIRST)
-        def _():
-            if level == 1:
-                block = at(z, xo)
-                arrived(block, c)
-                upward(block, c)
-                downward(block, c)
-                return
-            for sign, onward in ((1, downward), (-1, upward)):
-                far = z + sign * (level - 1)
-
-                @pl.when(inside(far))
-                def _():
-                    arrived(at(far, xo), c)
-                    onward(at(far, xo), c)
-
-    def sent(kind, block, start, stop):
-        if stop > start:
-            target = {UP: at(z + 1, x), DOWN: at(z - 1, x), ACROSS: at(z, xo)}[kind]
-            rows_of(kind, block, start * prow, (stop - start) * prow, target).wait_send()
+
+        if level == 1:
+            handed_on(lambda block, target_z: along(block, c, target_z))
+        for sign in (1, -1):
+            far = z + sign * level
+
+            @pl.when(inside(far))
+            def _():
+                across(at(far, x), c)
+
+    def sent(kind, block, target):
+        rows_of(kind, block, 0, tokens, target).wait_send()
 
     def all_sent(dist):
-        for sign, kind in ((1, DOWN), (-1, UP)):
+        if dist == 0:
+            sent(ACROSS, me, at(z, xo))
+            own_targets(lambda target_z: sent(target_z, me, at(target_z, x)))
+            return
+        if dist == 1:
+            handed_on(lambda block, target_z: sent(target_z, block, at(target_z, x)))
+        for sign in (1, -1):
             far = z + sign * dist
-            goes = z > 0 if kind == DOWN else z < ROWS_Z - 1
-
-            @pl.when(inside(far) & goes)
+
+            @pl.when(inside(far))
             def _():
-                sent(kind, at(far, x), 0, PIECES)
-                sent(kind, at(far, xo), 0, X_FIRST)
-
-            if dist > 0:
-                @pl.when(inside(far))
-                def _():
-                    sent(ACROSS, at(far, x), X_FIRST, PIECES)
-        if dist == 0:
-            sent(ACROSS, me, 0, PIECES)
+                sent(ACROSS, at(far, x), at(z, xo))
 
     def rest_of(block):
-        @pl.loop(X_FIRST, PIECES)
+        @pl.loop(0, PIECES)
         def _(c):
             arrived(block, c)
 
@@ -288,9 +283,8 @@
 
     @pl.loop(0, PIECES)
     def _(c):
+        own_targets(lambda target_z: along(me, c, target_z))
         across(me, c)
-        upward(me, c)
-        downward(me, c)
 
     for load in loads[1:]:
         load.wait()
@@ -403,14 +397,8 @@
 
     half = tokens // 2
     for part_no in range(2):
-        at_end = (z == 0) | (z == ROWS_Z - 1)
         for c in range(part_no * PIECES // 2, (part_no + 1) * PIECES // 2):
-            if c < X_FIRST:
-                @pl.when(at_end)
-                def _():
-                    arrived(last, c)
-            else:
-                arrived(last, c)
+            arrived(last, c)
         span = slice(part_no * half, (part_no + 1) * half)
         turn(last, part_no * half // ROWS, (part_no + 1) * half // ROWS)
 
@@ -552,7 +540,7 @@
             vmem((dpeers, 8, 2 * rank), f32),
             dma((10,)),
             dma((nmp,)),
-            dma((3, nmp)),
+            dma((ROWS_Z + 1, nmp)),
             dma((nmp, PIECES)),
             dma((peers,)), dma((peers,)),
             dma((peers,)), dma((peers,)),

time: 84.4 us -> 88.6 us (1.050)
  Pallas kernels: 82.8 us -> 87 us
    pallas_call x1, Pallas kernels: 82.8 us -> 87 us  [fused_device(): pl.pallas_call(functools.partial(fused_kernel, ndp, nmp), out_shape=jax.S...]
where the time goes in v4:
time: 88.6 us; the launch traced here: 88.4 us
  Pallas kernels  87 us (98%)
  local copies, waits for them, and re-layouts  1.42 us (2%)
    pallas_call x1, Pallas kernels, fused_device(): pl.pallas_call(functools.partial(fused_kernel, ndp, nmp), out_shape=jax.S...  87 us

profile of v4, /device:TPU:0, one launch (start us, length us, event | category | flops | bytes accessed | tf_op | source)
XLA Modules:
  0.0 88.4 jit_solution(3810567554212801684)
XLA Ops:
  0.0 87.0 %shard_map.109 = f32[3,8,512]{2,1,0:T(8,128)} custom-call(bf16[512,512]{1,0:T(8,128)(2,1)} %x_hbm.1, bf16[512,1792]{1,0:T(8,128)(2,1)} %gate_hbm.1, bf16[512,1792]{1,0:T(8,128)(2,1)} %up_hbm.1, bf16[512,512]{1,0:T(8,128)(2,1)} %grad_hbm.1, bf16[1792,4096]{1,0:T(8,128)(2,1)} %w_hbm.1, bf16[64,512]{1,0:T(8,128)(2,1)} %bitcast.9, bf16[64,1792]{1,0:T(8,128)(2,1)} %bitcast.6, ...), custom_call_target="tpu_custom_call" | custom-call | flops 7516192768 | bytes 14680064 | tf_op jit(solution)/shard_map/pallas_call | solution.py:504
  87.0 1.4 %copy.13 = f32[8,3,512]{2,0,1:T(8,128)} copy(f32[8,3,512]{2,0,1:T(8,128)} %bitcast.5) | data formatting | bytes 98304

commit v5 on v3

--- a/solution.py
+++ b/solution.py
@@ -107,9 +107,9 @@
     out_ref,
     x_v, gate_v, up_v, grad_v, w_v, pin_v, phid_v, pgate_v, pup_v, pout_v, seq_v,
     grad_t, hgrad, act, upslope, hid_tile, up_tile, acc_hid, acc_a, acc_b,
-    fac_send, fac_recv, full, weighted, raw_own, raw_send, raw_recv,
+    fac_send, fac_recv, pair_send, pair_recv, hid_own, raw_down_v, full, weighted, raw_own, raw_send, raw_recv,
     sq_mine, sq_recv, sq_group, sq_dp,
-    load_sem, w_sem, g_send, g_recv, fac_ss, fac_rs, full_ss, full_rs, raw_ss, raw_rs,
+    load_sem, w_sem, g_send, g_recv, fac_ss, fac_rs, pair_ss, pair_rs, full_ss, full_rs, raw_ss, raw_rs,
     sq_ss, sq_rs, dp_ss, dp_rs,
 ):
     dp = lax.axis_index("dp")
@@ -182,6 +182,14 @@
     def inside(far):
         return (far >= 0) & (far < ROWS_Z)
 
+    per_turn = max(ROWS // prow, 1)
+
+    def turn(block, low=0, high=tokens // ROWS):
+        @pl.loop(low, high)
+        def _(r):
+            rows = pl.ds(pl.multiple_of(r * ROWS, ROWS), ROWS)
+            grad_t[block, :, rows] = grad_v[block, rows, :].T
+
     def pass_on(level, c):
         for sign, onward in ((1, downward), (-1, upward)):
             far = z + sign * level
@@ -194,6 +202,10 @@
                 @pl.when(c >= X_FIRST)
                 def _():
                     across(at(far, x), c)
+
+                @pl.when(lax.rem(c, per_turn) == per_turn - 1)
+                def _():
+                    turn(at(far, x), c // per_turn, c // per_turn + 1)
 
         @pl.when(c < X_FIRST)
         def _():
@@ -238,12 +250,6 @@
         def _(c):
             arrived(block, c)
 
-    def turn(block, low=0, high=tokens // ROWS):
-        @pl.loop(low, high)
-        def _(r):
-            rows = pl.ds(pl.multiple_of(r * ROWS, ROWS), ROWS)
-            grad_t[block, :, rows] = grad_v[block, rows, :].T
-
     def add_block(block, low, high, first=False):
         @pl.loop(low, high)
         def _(n):
@@ -280,7 +286,7 @@
             rest_of(block)
             turn(block)
 
-        level_blocks(level, turn, whole)
+        level_blocks(level, lambda block: None, whole)
 
     def add_level(level, low, high):
         add = lambda block: add_block(block, low, high)
@@ -297,7 +303,7 @@
     turn(me)
     out_t = jnp.dot(pout_v[...], grad_t[me], preferred_element_type=f32)
     for p in range(nmp):
-        fac_send[p, 2 * own:3 * own, :] = out_t[p * own:(p + 1) * own, :]
+        pair_send[p, own:2 * own, :] = out_t[p * own:(p + 1) * own, :].astype(bf16)
     in_t = lax.dot_general(pin_v[...], x_v[...], NT, preferred_element_type=f32)
     for p in range(nmp):
         fac_send[p, 0:own, :] = in_t[p * own:(p + 1) * own, :]
@@ -321,7 +327,7 @@
         acc_hid[...] += jnp.dot(phid_v[:, cols], hid_tile[...], preferred_element_type=f32)
 
     for p in range(nmp):
-        fac_send[p, own:2 * own, :] = acc_hid[p * own:(p + 1) * own, :]
+        pair_send[p, 0:own, :] = acc_hid[p * own:(p + 1) * own, :].astype(bf16)
 
     def exchange(src_of, dst, send_sems, recv_sems):
         return [
@@ -333,6 +339,7 @@
         ]
 
     fac_copies = exchange(lambda peer: fac_send.at[peer], fac_recv, fac_ss, fac_rs)
+    fac_copies += exchange(lambda peer: pair_send.at[peer], pair_recv, pair_ss, pair_rs)
     for copy in fac_copies:
         copy.start()
 
@@ -354,10 +361,12 @@
     for copy in fac_copies:
         copy.wait_recv()
     mine = fac_send[me]
+    pair = pair_send[me].astype(f32)
     for k in range(nmp - 1):
         mine = mine + fac_recv[k]
-    full[me] = jnp.concatenate([mine[0:own], mine[2 * own:3 * own]], axis=0).astype(bf16)
-    hid_own = mine[own:2 * own]
+        pair = pair + pair_recv[k].astype(f32)
+    full[me] = jnp.concatenate([mine, pair[own:]], axis=0).astype(bf16)
+    hid_own[...] = pair[:own]
     full_copies = [
         pltpu.make_async_remote_copy(
             src_ref=full.at[me], dst_ref=full.at[me], send_sem=full_ss.at[k], recv_sem=full_rs.at[k],
@@ -369,13 +378,10 @@
         copy.start()
     await_level(2)
 
-    @pl.loop(0, PIECES)
+    @pl.loop(0, PIECES // 2)
     def _(c):
         pass_on(3, c)
         add_level(2, *share(c))
-
-    await_level(3)
-    add_level(3, 0, tiles)
 
     for copy in full_copies:
         copy.wait_recv()
@@ -392,9 +398,18 @@
     hid_high = weighted_hid.astype(bf16)
     hid_low = (weighted_hid - hid_high.astype(f32)).astype(bf16)
     out_bf = out_full.astype(bf16)
-    raw_down = lax.dot_general(hid_high, out_bf, NT, preferred_element_type=f32) + lax.dot_general(
+    raw_down_v[...] = lax.dot_general(hid_high, out_bf, NT, preferred_element_type=f32) + lax.dot_general(
         hid_low, out_bf, NT, preferred_element_type=f32
     )
+
+    @pl.loop(PIECES // 2, PIECES)
+    def _(c):
+        pass_on(3, c)
+        add_level(2, *share(c))
+
+    await_level(3)
+    add_level(3, 0, tiles)
+
     all_sent(0)
     all_sent(1)
 
@@ -453,6 +468,8 @@
     raw = raw_own[me]
     for k in range(nmp - 1):
         raw = raw + raw_recv[k].astype(f32)
+
+    raw_down = raw_down_v[...]
 
     sq_pair = jnp.sum(raw * raw, axis=0, keepdims=True)
     sq_down = jnp.sum(raw_down * raw_down, axis=0, keepdims=True)
@@ -539,8 +556,12 @@
             vmem((rank, tokens), f32),
             vmem((rank, tokens), f32),
             vmem((rank, tokens), f32),
-            vmem((nmp, 3 * own, tokens), f32),
-            vmem((peers, 3 * own, tokens), f32),
+            vmem((nmp, own, tokens), f32),
+            vmem((peers, own, tokens), f32),
+            vmem((nmp, 2 * own, tokens), bf16),
+            vmem((peers, 2 * own, tokens), bf16),
+            vmem((own, tokens), f32),
+            vmem((own * SEQ_DEV, rank), f32),
             vmem((nmp, 2 * own, tokens), bf16),
             vmem((nmp, own * SEQ_DEV, tokens), bf16),
             vmem((nmp, own * SEQ_DEV, 2 * rank), f32),
@@ -558,6 +579,7 @@
             dma((peers,)), dma((peers,)),
             dma((peers,)), dma((peers,)),
             dma((peers,)), dma((peers,)),
+            dma((peers,)), dma((peers,)),
             dma((dpeers,)), dma((dpeers,)),
         ],
         compiler_params=pltpu.CompilerParams(

time: 84.4 us -> 84.8 us (level)
  no operation moved by 1% of the time
where the time goes in v5:
time: 84.8 us; the launch traced here: 84.7 us
  Pallas kernels  83.2 us (98%)
  local copies, waits for them, and re-layouts  1.42 us (2%)
    pallas_call x1, Pallas kernels, fused_device(): pl.pallas_call(functools.partial(fused_kernel, ndp, nmp), out_shape=jax.S...  83.2 us

profile of v5, /device:TPU:0, one launch (start us, length us, event | category | flops | bytes accessed | tf_op | source)
XLA Modules:
  0.0 84.7 jit_solution(15388663409704484312)
XLA Ops:
  0.0 83.2 %shard_map.109 = f32[3,8,512]{2,1,0:T(8,128)} custom-call(bf16[512,512]{1,0:T(8,128)(2,1)} %x_hbm.1, bf16[512,1792]{1,0:T(8,128)(2,1)} %gate_hbm.1, bf16[512,1792]{1,0:T(8,128)(2,1)} %up_hbm.1, bf16[512,512]{1,0:T(8,128)(2,1)} %grad_hbm.1, bf16[1792,4096]{1,0:T(8,128)(2,1)} %w_hbm.1, bf16[64,512]{1,0:T(8,128)(2,1)} %bitcast.9, bf16[64,1792]{1,0:T(8,128)(2,1)} %bitcast.6, ...), custom_call_target="tpu_custom_call" | custom-call | flops 7516192768 | bytes 14680064 | tf_op jit(solution)/shard_map/pallas_call | solution.py:533
  83.2 1.4 %copy.13 = f32[8,3,512]{2,0,1:T(8,128)} copy(f32[8,3,512]{2,0,1:T(8,128)} %bitcast.5) | data formatting | bytes 98304

commit v6 on v5

--- a/solution.py
+++ b/solution.py
@@ -107,9 +107,9 @@
     out_ref,
     x_v, gate_v, up_v, grad_v, w_v, pin_v, phid_v, pgate_v, pup_v, pout_v, seq_v,
     grad_t, hgrad, act, upslope, hid_tile, up_tile, acc_hid, acc_a, acc_b,
-    fac_send, fac_recv, pair_send, pair_recv, hid_own, raw_down_v, full, weighted, raw_own, raw_send, raw_recv,
+    fac_send, fac_recv, full, weighted, raw_down_v, raw_own, raw_send, raw_recv,
     sq_mine, sq_recv, sq_group, sq_dp,
-    load_sem, w_sem, g_send, g_recv, fac_ss, fac_rs, pair_ss, pair_rs, full_ss, full_rs, raw_ss, raw_rs,
+    load_sem, w_sem, g_send, g_recv, fac_ss, fac_rs, full_ss, full_rs, raw_ss, raw_rs,
     sq_ss, sq_rs, dp_ss, dp_rs,
 ):
     dp = lax.axis_index("dp")
@@ -303,7 +303,7 @@
     turn(me)
     out_t = jnp.dot(pout_v[...], grad_t[me], preferred_element_type=f32)
     for p in range(nmp):
-        pair_send[p, own:2 * own, :] = out_t[p * own:(p + 1) * own, :].astype(bf16)
+        fac_send[p, 2 * own:3 * own, :] = out_t[p * own:(p + 1) * own, :]
     in_t = lax.dot_general(pin_v[...], x_v[...], NT, preferred_element_type=f32)
     for p in range(nmp):
         fac_send[p, 0:own, :] = in_t[p * own:(p + 1) * own, :]
@@ -312,6 +312,10 @@
     @pl.loop(0, tiles)
     def _(n):
         cols = pl.ds(pl.multiple_of(n * TILE, TILE), TILE)
+
+        @pl.when(n < PIECES)
+        def _():
+            pass_on(1, n)
 
         @pl.loop(0, tokens // ROWS)
         def _(r):
@@ -327,7 +331,7 @@
         acc_hid[...] += jnp.dot(phid_v[:, cols], hid_tile[...], preferred_element_type=f32)
 
     for p in range(nmp):
-        pair_send[p, 0:own, :] = acc_hid[p * own:(p + 1) * own, :].astype(bf16)
+        fac_send[p, own:2 * own, :] = acc_hid[p * own:(p + 1) * own, :]
 
     def exchange(src_of, dst, send_sems, recv_sems):
         return [
@@ -339,34 +343,30 @@
         ]
 
     fac_copies = exchange(lambda peer: fac_send.at[peer], fac_recv, fac_ss, fac_rs)
-    fac_copies += exchange(lambda peer: pair_send.at[peer], pair_recv, pair_ss, pair_rs)
     for copy in fac_copies:
         copy.start()
 
+    @pl.loop(min(tiles, PIECES), PIECES)
+    def _(c):
+        pass_on(1, c)
+
     for load in w_loads:
         load.wait()
-
-    @pl.loop(0, PIECES)
-    def _(c):
-        pass_on(1, c)
-        add_block(me, *share(c), first=True)
-
-    await_level(1)
 
     @pl.loop(0, PIECES)
     def _(c):
         pass_on(2, c)
-        add_level(1, *share(c))
+        add_block(me, *share(c), first=True)
+
+    await_level(1)
 
     for copy in fac_copies:
         copy.wait_recv()
     mine = fac_send[me]
-    pair = pair_send[me].astype(f32)
     for k in range(nmp - 1):
         mine = mine + fac_recv[k]
-        pair = pair + pair_recv[k].astype(f32)
-    full[me] = jnp.concatenate([mine, pair[own:]], axis=0).astype(bf16)
-    hid_own[...] = pair[:own]
+    full[me] = jnp.concatenate([mine[0:own], mine[2 * own:3 * own]], axis=0).astype(bf16)
+    hid_own = mine[own:2 * own]
     full_copies = [
         pltpu.make_async_remote_copy(
             src_ref=full.at[me], dst_ref=full.at[me], send_sem=full_ss.at[k], recv_sem=full_rs.at[k],
@@ -376,12 +376,10 @@
     ]
     for copy in full_copies:
         copy.start()
-    await_level(2)
-
     @pl.loop(0, PIECES // 2)
     def _(c):
         pass_on(3, c)
-        add_level(2, *share(c))
+        add_level(1, *share(c))
 
     for copy in full_copies:
         copy.wait_recv()
@@ -405,8 +403,10 @@
     @pl.loop(PIECES // 2, PIECES)
     def _(c):
         pass_on(3, c)
-        add_level(2, *share(c))
-
+        add_level(1, *share(c))
+
+    await_level(2)
+    add_level(2, 0, tiles)
     await_level(3)
     add_level(3, 0, tiles)
 
@@ -556,14 +556,11 @@
             vmem((rank, tokens), f32),
             vmem((rank, tokens), f32),
             vmem((rank, tokens), f32),
-            vmem((nmp, own, tokens), f32),
-            vmem((peers, own, tokens), f32),
-            vmem((nmp, 2 * own, tokens), bf16),
-            vmem((peers, 2 * own, tokens), bf16),
-            vmem((own, tokens), f32),
-            vmem((own * SEQ_DEV, rank), f32),
+            vmem((nmp, 3 * own, tokens), f32),
+            vmem((peers, 3 * own, tokens), f32),
             vmem((nmp, 2 * own, tokens), bf16),
             vmem((nmp, own * SEQ_DEV, tokens), bf16),
+            vmem((own * SEQ_DEV, rank), f32),
             vmem((nmp, own * SEQ_DEV, 2 * rank), f32),
             vmem((nmp, own * SEQ_DEV, 2 * rank), bf16),
             vmem((peers, own * SEQ_DEV, 2 * rank), bf16),
@@ -575,7 +572,6 @@
             dma((nmp,)),
             dma((3, nmp)),
             dma((nmp, PIECES)),
-            dma((peers,)), dma((peers,)),
             dma((peers,)), dma((peers,)),
             dma((peers,)), dma((peers,)),
             dma((peers,)), dma((peers,)),

time: 84.8 us -> 91.6 us (1.080)
  Pallas kernels: 83.2 us -> 90 us
    pallas_call x1, Pallas kernels: 83.2 us -> 90 us  [fused_device(): pl.pallas_call(functools.partial(fused_kernel, ndp, nmp), out_shape=jax.S...]
where the time goes in v6:
time: 91.6 us; the launch traced here: 91.5 us
  Pallas kernels  90 us (98%)
  local copies, waits for them, and re-layouts  1.42 us (2%)
    pallas_call x1, Pallas kernels, fused_device(): pl.pallas_call(functools.partial(fused_kernel, ndp, nmp), out_shape=jax.S...  90 us

profile of v6, /device:TPU:0, one launch (start us, length us, event | category | flops | bytes accessed | tf_op | source)
XLA Modules:
  0.0 91.5 jit_solution(3761367049347805562)
XLA Ops:
  0.0 90.0 %shard_map.109 = f32[3,8,512]{2,1,0:T(8,128)} custom-call(bf16[512,512]{1,0:T(8,128)(2,1)} %x_hbm.1, bf16[512,1792]{1,0:T(8,128)(2,1)} %gate_hbm.1, bf16[512,1792]{1,0:T(8,128)(2,1)} %up_hbm.1, bf16[512,512]{1,0:T(8,128)(2,1)} %grad_hbm.1, bf16[1792,4096]{1,0:T(8,128)(2,1)} %w_hbm.1, bf16[64,512]{1,0:T(8,128)(2,1)} %bitcast.9, bf16[64,1792]{1,0:T(8,128)(2,1)} %bitcast.6, ...), custom_call_target="tpu_custom_call" | custom-call | flops 7516192768 | bytes 14680064 | tf_op jit(solution)/shard_map/pallas_call | solution.py:533
  90.1 1.4 %copy.13 = f32[8,3,512]{2,0,1:T(8,128)} copy(f32[8,3,512]{2,0,1:T(8,128)} %bitcast.5) | data formatting | bytes 98304

commit v7 on v6

--- a/solution.py
+++ b/solution.py
@@ -95,7 +95,8 @@
 ROWS_Z, COLS_X = 4, 2
 PIECES = 8
 X_FIRST = 1
-TILE = 256
+TILE = 896
+UNITS = 128
 ROWS = 128
 NT = (((1,), (1,)), ((), ()))
 UP, DOWN, ACROSS = 0, 1, 2
@@ -121,6 +122,7 @@
     rank = pin_hbm.shape[0]
     own = rank // nmp
     prow = tokens // PIECES
+    half = tokens // 2
     f32, bf16 = jnp.float32, jnp.bfloat16
 
     def at(zz, xx):
@@ -313,20 +315,19 @@
     def _(n):
         cols = pl.ds(pl.multiple_of(n * TILE, TILE), TILE)
 
-        @pl.when(n < PIECES)
-        def _():
-            pass_on(1, n)
-
-        @pl.loop(0, tokens // ROWS)
-        def _(r):
-            rows = pl.ds(pl.multiple_of(r * ROWS, ROWS), ROWS)
-            g = gate_v[rows, cols].T.astype(f32)
-            u = up_v[rows, cols].T.astype(f32)
-            sig = 1.0 / (1.0 + jnp.exp(-g))
-            a = g * sig
-            act[n, :, rows] = a
-            upslope[n, :, rows] = u * (sig * (1.0 + g * (1.0 - sig)))
-            hid_tile[:, rows] = (a * u).astype(bf16)
+        @pl.loop(0, TILE // UNITS)
+        def _(k):
+            for r in range(tokens // half):
+                rows = slice(r * half, (r + 1) * half)
+                units = pl.ds(pl.multiple_of(k * UNITS, UNITS), UNITS)
+                lanes = pl.ds(pl.multiple_of(n * TILE + k * UNITS, UNITS), UNITS)
+                g = gate_v[rows, lanes].T.astype(f32)
+                u = up_v[rows, lanes].T.astype(f32)
+                sig = 1.0 / (1.0 + jnp.exp(-g))
+                a = g * sig
+                act[n, units, rows] = a
+                upslope[n, units, rows] = u * (sig * (1.0 + g * (1.0 - sig)))
+                hid_tile[units, rows] = (a * u).astype(bf16)
 
         acc_hid[...] += jnp.dot(phid_v[:, cols], hid_tile[...], preferred_element_type=f32)
 
@@ -346,19 +347,20 @@
     for copy in fac_copies:
         copy.start()
 
-    @pl.loop(min(tiles, PIECES), PIECES)
+    for load in w_loads:
+        load.wait()
+
+    @pl.loop(0, PIECES)
     def _(c):
         pass_on(1, c)
-
-    for load in w_loads:
-        load.wait()
+        add_block(me, *share(c), first=True)
+
+    await_level(1)
 
     @pl.loop(0, PIECES)
     def _(c):
         pass_on(2, c)
-        add_block(me, *share(c), first=True)
-
-    await_level(1)
+        add_level(1, *share(c))
 
     for copy in fac_copies:
         copy.wait_recv()
@@ -376,10 +378,12 @@
     ]
     for copy in full_copies:
         copy.start()
+    await_level(2)
+
     @pl.loop(0, PIECES // 2)
     def _(c):
         pass_on(3, c)
-        add_level(1, *share(c))
+        add_level(2, *share(c))
 
     for copy in full_copies:
         copy.wait_recv()
@@ -403,10 +407,8 @@
     @pl.loop(PIECES // 2, PIECES)
     def _(c):
         pass_on(3, c)
-        add_level(1, *share(c))
-
-    await_level(2)
-    add_level(2, 0, tiles)
+        add_level(2, *share(c))
+
     await_level(3)
     add_level(3, 0, tiles)
 
@@ -416,7 +418,6 @@
     acc_a[...] = jnp.zeros_like(acc_a)
     acc_b[...] = jnp.zeros_like(acc_b)
 
-    half = tokens // 2
     for part_no in range(2):
         at_end = (z == 0) | (z == ROWS_Z - 1)
         for c in range(part_no * PIECES // 2, (part_no + 1) * PIECES // 2):
@@ -434,12 +435,12 @@
             cols = pl.ds(pl.multiple_of(n * TILE, TILE), TILE)
             hgrad[n, :, span] += jnp.dot(w_v[last, cols, :], grad_t[last, :, span], preferred_element_type=f32)
 
-            @pl.loop(part_no * half // ROWS, (part_no + 1) * half // ROWS)
-            def _(r):
-                rows = pl.ds(pl.multiple_of(r * ROWS, ROWS), ROWS)
-                h = hgrad[n, :, rows]
-                hid_tile[:, rows] = (h * upslope[n, :, rows]).astype(bf16)
-                up_tile[:, rows] = (h * act[n, :, rows]).astype(bf16)
+            @pl.loop(0, TILE // UNITS)
+            def _(k):
+                units = pl.ds(pl.multiple_of(k * UNITS, UNITS), UNITS)
+                h = hgrad[n, units, span]
+                hid_tile[units, span] = (h * upslope[n, units, span]).astype(bf16)
+                up_tile[units, span] = (h * act[n, units, span]).astype(bf16)
 
             acc_a[:, span] += jnp.dot(pgate_v[:, cols], hid_tile[:, span], preferred_element_type=f32)
             acc_b[:, span] += jnp.dot(pup_v[:, cols], up_tile[:, span], preferred_element_type=f32)

time: 91.6 us -> 80.4 us (0.88)
  Pallas kernels: 90 us -> 78.8 us
    pallas_call x1, Pallas kernels: 90 us -> 78.8 us  [fused_device(): pl.pallas_call(functools.partial(fused_kernel, ndp, nmp), out_shape=jax.S...]
where the time goes in v7:
time: 80.4 us; the launch traced here: 80.2 us
  Pallas kernels  78.8 us (98%)
  local copies, waits for them, and re-layouts  1.42 us (2%)
    pallas_call x1, Pallas kernels, fused_device(): pl.pallas_call(functools.partial(fused_kernel, ndp, nmp), out_shape=jax.S...  78.8 us

profile of v7, /device:TPU:0, one launch (start us, length us, event | category | flops | bytes accessed | tf_op | source)
XLA Modules:
  0.0 80.2 jit_solution(17156719523832716668)
XLA Ops:
  0.0 78.8 %shard_map.109 = f32[3,8,512]{2,1,0:T(8,128)} custom-call(bf16[512,512]{1,0:T(8,128)(2,1)} %x_hbm.1, bf16[512,1792]{1,0:T(8,128)(2,1)} %gate_hbm.1, bf16[512,1792]{1,0:T(8,128)(2,1)} %up_hbm.1, bf16[512,512]{1,0:T(8,128)(2,1)} %grad_hbm.1, bf16[1792,4096]{1,0:T(8,128)(2,1)} %w_hbm.1, bf16[64,512]{1,0:T(8,128)(2,1)} %bitcast.9, bf16[64,1792]{1,0:T(8,128)(2,1)} %bitcast.6, ...), custom_call_target="tpu_custom_call" | custom-call | flops 7516192768 | bytes 14680064 | tf_op jit(solution)/shard_map/pallas_call | solution.py:534
  78.8 1.4 %copy.13 = f32[8,3,512]{2,0,1:T(8,128)} copy(f32[8,3,512]{2,0,1:T(8,128)} %bitcast.5) | data formatting | bytes 98304
